TPU v7x, 32 devices: a whole 2x2x4 slice. The times are simulated.
32 devices in a mesh: groups: 2 (over x), ctx: 16 (over z, y, core).
Axes of the slice: x: 2, y: 2, z: 4, core: 2. Of those that a mesh axis runs over, the one named last changes fastest.
Arguments:
- queries: bfloat16 [4096, 4096], P(('groups', 'ctx')), parts along dimension 0, may hold values from -600 to 600
- keys: bfloat16 [4096, 512], P(('groups', 'ctx')), parts along dimension 0, may hold values from -600 to 600
- values: bfloat16 [4096, 512], P(('groups', 'ctx')), parts along dimension 0, may hold values from -6 to 6
- q_gain: float32 [128], replicated, may hold values from 0.5 to 6
- k_gain: float32 [128], replicated, may hold values from 0.5 to 6
- lengths: int32 [32], P('groups'), parts along dimension 0, may hold values from 1 to 1024, as said below
- placing: int32 [32, 8], P(('groups', 'ctx')), parts along dimension 0, may hold values from 0 to 15, as said below
- owners: int32 [32], P('groups'), parts along dimension 0, may hold values from 0 to 15, as said below
Outputs:
- attended: bfloat16 [4096, 4096], P(('groups', 'ctx')), parts along dimension 0
- kv_cache: bfloat16 [40960, 1024], P(('groups', 'ctx')), parts along dimension 0
There are 2 independent parts, one for each index of `groups`. A program takes and returns all parts, laid end to end along the dimension named above; an argument that names none is the same for every part. Nothing has to cross between parts.
Inputs may be any that keep to these rules, and one draw needn't show every extreme that they name: The 16 lengths sum to 2048; one of them is exactly 1024. `placing`: row s lists the 8 devices of the aligned group of 8 devices that holds s, each once; every device receives one block from each device of its group. owners[i] is a device that holds at least one row of session i and lies at most 1 device before the device that holds its last row.
All inputs are finite; a program needn't handle non-finite values.
Results may differ from a plain program's by a relative error of at most 0.0025.
The roundings to bfloat16 on the way count: a program that leaves them out, or rounds other values in their place, can miss the bound.
Values may be sent and summed in bfloat16 or wider, within the bound.
A program may use at most 192 MiB of HBM per device.

v0:
```python
import jax
import jax.numpy as jnp
from jax import lax
from jax.sharding import PartitionSpec as P

HD = 128
TRADE = 8


EPS = 1e-06
THETA = 1000000.0


def partner(block, axis, distance):
    count = lax.axis_size(axis)
    route = []
    for low in range(count):
        high = low | 1 << distance
        if high != low and high < count:
            route += [(low, high), (high, low)]
    return lax.ppermute(block, axis, route)


def session_ids(rows, starts):
    return jnp.sum((rows[:, None] >= starts[None, :]).astype(jnp.int32), axis=1) - 1


def rotate(block, gain, places):
    count = block.shape[0]
    heads = block.shape[1] // HD
    entries = block.astype(jnp.float32).reshape(count, heads, HD)
    mean_sq = jnp.mean(entries * entries, axis=-1, keepdims=True)
    normed = entries * lax.rsqrt(mean_sq + EPS) * gain
    half = HD // 2
    freqs = jnp.power(jnp.float32(THETA), -jnp.arange(0, HD, 2).astype(jnp.float32) / HD)
    angles = places.astype(jnp.float32)[:, None] * freqs[None, :]
    cosine = jnp.cos(angles)[:, None, :]
    sine = jnp.sin(angles)[:, None, :]
    first = normed[..., :half]
    second = normed[..., half:]
    turned = jnp.concatenate(
        [first * cosine - second * sine, second * cosine + first * sine], axis=-1
    )
    return turned.reshape(count, heads * HD).astype(jnp.bfloat16)


def block_width(count):
    for candidate in range(512, 0, -1):
        if count % candidate == 0:
            return candidate
    return count


def body(queries, keys, values, q_gain, k_gain, lengths, placing, owners):
    rows_dev = queries.shape[0]
    kv_heads = keys.shape[1] // HD
    q_heads = queries.shape[1] // HD
    group = q_heads // kv_heads
    unit = rows_dev // TRADE
    devices = lax.axis_size("ctx")
    device = lax.axis_index("ctx")
    reach = devices // 2
    lead = devices // 16
    cache_rows = (reach + lead + 1) * rows_dev
    tables = lengths.shape[0]
    session_index = jnp.arange(tables, dtype=jnp.int32)
    starts = jnp.cumsum(lengths) - lengths
    own_rows = device * rows_dev + jnp.arange(rows_dev, dtype=jnp.int32)
    own_sessions = session_ids(own_rows, starts)
    own_starts = jnp.sum(
        jnp.where(own_sessions[:, None] == session_index[None, :], starts[None, :], 0), axis=1
    )
    places = own_rows - own_starts
    q_rot = rotate(queries, q_gain, places)
    k_rot = rotate(keys, k_gain, places)
    key_vals = jnp.concatenate([k_rot, values], axis=1)
    q_units = q_rot.reshape(TRADE, unit, q_heads * HD)
    row_units = own_rows.reshape(TRADE, unit)
    targets = placing[0]
    held_q, held_rows, held_dest = (q_units, row_units, targets)
    half = TRADE // 2
    for bit in range(TRADE.bit_length() - 1):
        mine = device // (1 << bit) % 2
        away = (held_dest // (1 << bit) % 2 != mine).astype(jnp.int32)
        order = jnp.argsort(away, stable=True)
        keep_idx = order[:half]
        move_idx = order[half:]
        moved_q, moved_rows, moved_dest = partner(
            (held_q[move_idx], held_rows[move_idx], held_dest[move_idx]), "ctx", bit
        )
        held_q = jnp.concatenate([held_q[keep_idx], moved_q], axis=0)
        held_rows = jnp.concatenate([held_rows[keep_idx], moved_rows], axis=0)
        held_dest = jnp.concatenate([held_dest[keep_idx], moved_dest], axis=0)
    order = jnp.argsort(held_rows[:, 0] // rows_dev, stable=True)
    got_q = held_q[order]
    got_rows = held_rows[order]
    q_rows = got_rows.reshape(rows_dev)
    q_sessions = session_ids(q_rows, starts)
    query_heads = got_q.reshape(rows_dev, kv_heads, group, HD)
    scale = 1.0 / HD**0.5
    window_start = (device - reach) * rows_dev

    def absorb(state, block):
        peak, total, summed = state
        k_blk, v_blk, k_rows, present = block
        k_sessions = session_ids(k_rows, starts)
        mask = (
            (k_sessions[None, :] == q_sessions[:, None])
            & (k_rows[None, :] <= q_rows[:, None])
            & present[None, :]
        )
        scores = (
            jnp.einsum("qkgd,nkd->kgqn", query_heads, k_blk, preferred_element_type=jnp.float32)
            * scale
        )
        scores = jnp.where(mask, scores, -1e30)
        new_peak = jnp.maximum(peak, jnp.max(scores, axis=-1))
        probs = jnp.where(mask, jnp.exp(scores - new_peak[..., None]), 0.0)
        factor = jnp.exp(peak - new_peak)
        total = total * factor + jnp.sum(probs, axis=-1)
        summed = summed * factor[..., None] + jnp.einsum(
            "kgqn,nkd->kgqd", probs.astype(jnp.bfloat16), v_blk, preferred_element_type=jnp.float32
        )
        return ((new_peak, total, summed), None)

    piece = lax.all_gather(key_vals, "ctx", axis=0, tiled=True)
    first = jnp.int32(0)
    present = jnp.ones((piece.shape[0],), jnp.bool_)
    count = piece.shape[0]
    k_rows = jnp.arange(count, dtype=jnp.int32)
    peak = jnp.full((kv_heads, group, rows_dev), -1e30, jnp.float32)
    total = jnp.zeros((kv_heads, group, rows_dev), jnp.float32)
    summed = jnp.zeros((kv_heads, group, rows_dev, HD), jnp.float32)
    cache = jnp.zeros((cache_rows, key_vals.shape[1]), jnp.bfloat16)
    k_sessions = session_ids(k_rows, starts)
    low_session = jnp.min(jnp.where(present, k_sessions, tables))
    high_session = jnp.max(jnp.where(present, k_sessions, -1))
    needed = jnp.any((q_sessions >= low_session) & (q_sessions <= high_session) & (q_rows >= first))
    width = block_width(count)
    blocks = count // width

    def attend(state):
        k_part = piece[:, : kv_heads * HD].reshape(blocks, width, kv_heads, HD)
        v_part = piece[:, kv_heads * HD :].reshape(blocks, width, kv_heads, HD)
        state, unused = lax.scan(
            absorb,
            state,
            (k_part, v_part, k_rows.reshape(blocks, width), present.reshape(blocks, width)),
        )
        return state

    peak, total, summed = lax.cond(needed, attend, lambda state: state, (peak, total, summed))
    owner_of = jnp.sum(
        jnp.where(k_sessions[:, None] == session_index[None, :], owners[None, :], 0), axis=1
    )
    owned = present & (owner_of == device)

    def place(stored):
        masked = jnp.where(owned[:, None], piece, jnp.zeros_like(piece))
        padded = jnp.pad(stored, ((count, count), (0, 0)))
        at = jnp.clip(first - window_start + count, 0, cache_rows + count)
        region = lax.dynamic_slice_in_dim(padded, at, count, 0)
        padded = lax.dynamic_update_slice_in_dim(padded, region + masked, at, 0)
        return padded[count : count + cache_rows]

    cache = lax.cond(jnp.any(owned), place, lambda stored: stored, cache)
    carry = (peak, total, summed, cache)
    peak, total, summed, cache = carry
    attended = (
        (summed / total[..., None])
        .transpose(2, 0, 1, 3)
        .reshape(rows_dev, q_heads * HD)
        .astype(jnp.bfloat16)
    )
    return (attended, cache)


def solution(mesh):
    return jax.shard_map(
        body,
        mesh=mesh,
        in_specs=(
            P(("groups", "ctx"), None),
            P(("groups", "ctx"), None),
            P(("groups", "ctx"), None),
            P(),
            P(),
            P("groups"),
            P(("groups", "ctx"), None),
            P("groups"),
        ),
        out_specs=(P(("groups", "ctx"), None), P(("groups", "ctx"), None)),
        check_vma=False,
    )
```

profile of v0, /device:TPU:12, one launch (start us, length us, event | category | flops | bytes accessed | tf_op | source)
XLA Modules:
  0.0 195.5 jit_solution(5440241956885238726)
XLA Ops:
  19.3 3.0 %collective-permute-done.3 = s32[4]{0:T(128)S(1)} collective-permute-done((s32[4]{0:T(128)S(1)}, s32[4]{0:T(128)S(1)}, u32[]{:S(2)}, u32[]{:S(2)}) %collective-permute-start.3) | collective-permute-done | bytes 48 | tf_op jit(solution)/shard_map/ppermute | solution.py:21
  25.2 2.5 %collective-permute-done.2 = s32[4,16]{1,0:T(4,128)S(1)} collective-permute-done((s32[4,16]{1,0:T(4,128)S(1)}, s32[4,16]{1,0:T(4,128)S(1)}, u32[]{:S(2)}, u32[]{:S(2)}) %collective-permute-start.2) | collective-permute-done | bytes 288 | tf_op jit(solution)/shard_map/ppermute | solution.py:21
  29.4 2.6 %collective-permute-done.4 = s32[4,16]{1,0:T(4,128)S(1)} collective-permute-done((s32[4,16]{1,0:T(4,128)S(1)}, s32[4,16]{1,0:T(4,128)S(1)}, u32[]{:S(2)}, u32[]{:S(2)}) %collective-permute-start.4) | collective-permute-done | bytes 288 | tf_op jit(solution)/shard_map/ppermute | solution.py:21
  45.0 15.5 %collective-permute-done.6 = bf16[4,16,4096]{2,1,0:T(8,128)(2,1)S(1)} collective-permute-done((bf16[4,16,4096]{2,1,0:T(8,128)(2,1)S(1)}, bf16[4,16,4096]{2,1,0:T(8,128)(2,1)S(1)}, u32[]{:S(2)}, u32[]{:S(2)}) %collective-permute-start.6) | collective-permute-done | bytes 524320 | tf_op jit(solution)/shard_map/ppermute | solution.py:21
  63.6 2.0 %and_reduce_fusion = pred[]{:T(512)} fusion(s32[128]{0:T(128)S(1)} %ge.86, s32[128]{0:T(128)S(1)} %get-tuple-element.285, s32[]{:T(128)} %get-tuple-element.283, s32[]{:T(128)} %get-tuple-element.282), kind=kLoop, calls=%fused_computation.107 | loop fusion | flops 895 | bytes 1033 | tf_op jit(solution)/shard_map/reduce_or | solution.py:138
  66.9 20.9 %collective-permute-done.7 = bf16[4,16,4096]{2,1,0:T(8,128)(2,1)S(1)} collective-permute-done((bf16[4,16,4096]{2,1,0:T(8,128)(2,1)S(1)}, bf16[4,16,4096]{2,1,0:T(8,128)(2,1)S(1)}, u32[]{:S(2)}, u32[]{:S(2)}) %collective-permute-start.7) | collective-permute-done | bytes 524320 | tf_op jit(solution)/shard_map/ppermute | solution.py:21
  87.9 5.9 %all-gather.2.cloned.1.call-done = bf16[2048,1024]{1,0:T(8,128)(2,1)} async-done(((bf16[128,1024]{1,0:T(8,128)(2,1)}), bf16[2048,1024]{1,0:T(8,128)(2,1)}) %all-gather.2.cloned.1.call-update) | async-done | bytes 4194320 | tf_op jit(solution)/shard_map/all_gather | solution.py:126
  93.8 57.8 %conditional.2 = (f32[4,8,128]{2,1,0:T(8,128)}, f32[4,8,128,128]{3,2,1,0:T(8,128)}) conditional(s32[]{:T(128)} %convert_element_type.79, () %tuple.37, (bf16[2048,1024]{1,0:T(8,128)(2,1)}, s32[2048]{0:T(1024)S(1)}, s32[128]{0:T(128)S(1)}, bf16[8,16,4096]{2,1,0:T(8,128)(2,1)S(1)}, s32[8,1]{0,1:T(1,128)S(1)}, /*index=5*/s32[16]{0:T(128)S(1)}, ...), branch_computations={%region_14.15_spmd, %region_15.21_spmd} | conditional | flops 1102820480 | bytes 57189828 | solution.py:152
  95.2 4.4 %fusion.22 = (bf16[2048,512]{1,0:T(8,128)(2,1)}, bf16[2048,512]{1,0:T(8,128)(2,1)}) fusion(bf16[2048,1024]{1,0:T(8,128)(2,1)} %get-tuple-element.180), kind=kLoop, calls=%fused_computation.139 | loop fusion | bytes 8388608 | tf_op jit(solution)/shard_map/cond/branch_1_fun/slice | solution.py:144
  99.6 2.5 %reshape.168 = bf16[4,512,4,128]{3,2,1,0:T(4,128)(2,1)S(1)} reshape(bf16[2048,512]{1,0:T(8,128)(2,1)} %get-tuple-element.318) | data formatting | bytes 4194304 | tf_op jit(solution)/shard_map/cond/branch_1_fun/reshape | solution.py:144
  102.2 4.0 %reshape.166 = bf16[4,512,4,128]{3,2,1,0:T(4,128)(2,1)} reshape(bf16[2048,512]{1,0:T(8,128)(2,1)} %get-tuple-element.319) | data formatting | bytes 4194304 | tf_op jit(solution)/shard_map/cond/branch_1_fun/reshape | solution.py:143
  106.2 45.5 %while.17 = (s32[]{:T(128)}, f32[4,8,128]{2,1,0:T(8,128)S(1)}, f32[4,8,128]{2,1,0:T(8,128)}, f32[4,8,128,128]{3,2,1,0:T(8,128)}, s32[4,512]{1,0:T(4,128)S(1)}, /...) while((s32[]{:T(128)}, f32[4,8,128]{2,1,0:T(8,128)S(1)}, ...), condition=%wide.wide.region_20.20_spmd.clone, body=%wide.wide.region_16.19_spmd.clone.sunk | while | flops 1102819328 | bytes 34096352 | solution.py:145
  109.3 2.1 %fusion.39 = f32[4,8,128]{2,1,0:T(8,128)S(1)} fusion(f32[4,512,128,8]{2,1,3,0:T(8,128)S(1)} %get-tuple-element.466, f32[4,8,128]{2,1,0:T(8,128)S(1)} %select_maximum_fusion.3, pred[128,512]{0,1:T(8,128)(4,1)S(1)} %compare_and_fusion.3), kind=kLoop, calls=%fused_computation.24.clone.clone.1 | loop fusion | flops 10481664 | bytes 8486912 | tf_op jit(solution)/shard_map/cond/branch_1_fun/while/body/eval_jaxpr/reduce_sum | solution.py:120
  112.0 4.0 %fusion.41 = f32[4,8,128,128]{3,2,1,0:T(8,128)} fusion(f32[4,8,128,128]{3,2,1,0:T(8,128)} %get-tuple-element.487, f32[4,512,128,8]{2,1,3,0:T(8,128)S(1)} %get-tuple-element.466, f32[4,8,128]{2,1,0:T(8,128)S(1)} %select_maximum_fusion.3, pred[128,512]{0,1:T(8,128)(4,1)S(1)} %compare_and_fusion.3, f32[4,8,128]{2,1,0:T(8,128)S(1)} %get-tuple-element.468, ...), kind=kOutput, calls=%fused_computation.28.clone.clone.1 | convolution fusion | flops 548929536 | bytes 13205505 | tf_op jit(solution)/shard_map/cond/branch_1_fun/while/body/eval_jaxpr/kgqn,nkd->kgqd/dot_general | solution.py:121
  119.2 2.1 %fusion.39 = f32[4,8,128]{2,1,0:T(8,128)S(1)} fusion(f32[4,512,128,8]{2,1,3,0:T(8,128)S(1)} %get-tuple-element.466, f32[4,8,128]{2,1,0:T(8,128)S(1)} %select_maximum_fusion.3, pred[128,512]{0,1:T(8,128)(4,1)S(1)} %compare_and_fusion.3), kind=kLoop, calls=%fused_computation.24.clone.clone.1 | loop fusion | flops 10481664 | bytes 8486912 | tf_op jit(solution)/shard_map/cond/branch_1_fun/while/body/eval_jaxpr/reduce_sum | solution.py:120
  122.7 5.3 %fusion.41 = f32[4,8,128,128]{3,2,1,0:T(8,128)} fusion(f32[4,8,128,128]{3,2,1,0:T(8,128)} %get-tuple-element.487, f32[4,512,128,8]{2,1,3,0:T(8,128)S(1)} %get-tuple-element.466, f32[4,8,128]{2,1,0:T(8,128)S(1)} %select_maximum_fusion.3, pred[128,512]{0,1:T(8,128)(4,1)S(1)} %compare_and_fusion.3, f32[4,8,128]{2,1,0:T(8,128)S(1)} %get-tuple-element.468, ...), kind=kOutput, calls=%fused_computation.28.clone.clone.1 | convolution fusion | flops 548929536 | bytes 13205505 | tf_op jit(solution)/shard_map/cond/branch_1_fun/while/body/eval_jaxpr/kgqn,nkd->kgqd/dot_general | solution.py:121
  131.1 2.1 %fusion.39 = f32[4,8,128]{2,1,0:T(8,128)S(1)} fusion(f32[4,512,128,8]{2,1,3,0:T(8,128)S(1)} %get-tuple-element.466, f32[4,8,128]{2,1,0:T(8,128)S(1)} %select_maximum_fusion.3, pred[128,512]{0,1:T(8,128)(4,1)S(1)} %compare_and_fusion.3), kind=kLoop, calls=%fused_computation.24.clone.clone.1 | loop fusion | flops 10481664 | bytes 8486912 | tf_op jit(solution)/shard_map/cond/branch_1_fun/while/body/eval_jaxpr/reduce_sum | solution.py:120
  134.5 5.3 %fusion.41 = f32[4,8,128,128]{3,2,1,0:T(8,128)} fusion(f32[4,8,128,128]{3,2,1,0:T(8,128)} %get-tuple-element.487, f32[4,512,128,8]{2,1,3,0:T(8,128)S(1)} %get-tuple-element.466, f32[4,8,128]{2,1,0:T(8,128)S(1)} %select_maximum_fusion.3, pred[128,512]{0,1:T(8,128)(4,1)S(1)} %compare_and_fusion.3, f32[4,8,128]{2,1,0:T(8,128)S(1)} %get-tuple-element.468, ...), kind=kOutput, calls=%fused_computation.28.clone.clone.1 | convolution fusion | flops 548929536 | bytes 13205505 | tf_op jit(solution)/shard_map/cond/branch_1_fun/while/body/eval_jaxpr/kgqn,nkd->kgqd/dot_general | solution.py:121
  142.9 2.1 %fusion.39 = f32[4,8,128]{2,1,0:T(8,128)S(1)} fusion(f32[4,512,128,8]{2,1,3,0:T(8,128)S(1)} %get-tuple-element.466, f32[4,8,128]{2,1,0:T(8,128)S(1)} %select_maximum_fusion.3, pred[128,512]{0,1:T(8,128)(4,1)S(1)} %compare_and_fusion.3), kind=kLoop, calls=%fused_computation.24.clone.clone.1 | loop fusion | flops 10481664 | bytes 8486912 | tf_op jit(solution)/shard_map/cond/branch_1_fun/while/body/eval_jaxpr/reduce_sum | solution.py:120
  146.4 5.3 %fusion.41 = f32[4,8,128,128]{3,2,1,0:T(8,128)} fusion(f32[4,8,128,128]{3,2,1,0:T(8,128)} %get-tuple-element.487, f32[4,512,128,8]{2,1,3,0:T(8,128)S(1)} %get-tuple-element.466, f32[4,8,128]{2,1,0:T(8,128)S(1)} %select_maximum_fusion.3, pred[128,512]{0,1:T(8,128)(4,1)S(1)} %compare_and_fusion.3, f32[4,8,128]{2,1,0:T(8,128)S(1)} %get-tuple-element.468, ...), kind=kOutput, calls=%fused_computation.28.clone.clone.1 | convolution fusion | flops 548929536 | bytes 13205505 | tf_op jit(solution)/shard_map/cond/branch_1_fun/while/body/eval_jaxpr/kgqn,nkd->kgqd/dot_general | solution.py:121
  155.7 31.5 %conditional.3 = (bf16[1280,1024]{1,0:T(8,128)(2,1)S(1)}) conditional(s32[]{:T(128)} %convert_element_type.88, () %tuple.39, (s32[]{:T(128)}, pred[2048]{0:T(1024)(128)(4,1)S(1)}, bf16[2048,1024]{1,0:T(8,128)(2,1)}) %tuple.40), branch_computations={%region_23.24_spmd, %region_24.25_spmd} | conditional | flops 4194309 | bytes 33069648 | solution.py:166
  155.8 3.9 %select_add_fusion = bf16[2048,1024]{1,0:T(8,128)(2,1)} fusion(bf16[2048,1024]{1,0:T(8,128)(2,1)} %get-tuple-element.187, pred[2048]{0:T(1024)(128)(4,1)S(1)} %get-tuple-element.186, bf16[2048]{0:T(1024)(128)(2,1)S(1)} %pad_dynamic-slice_fusion), kind=kLoop, calls=%fused_computation.18 | loop fusion | flops 4194304 | bytes 8394752 | tf_op jit(solution)/shard_map/cond/branch_1_fun/add | solution.py:163
  159.7 4.9 %pad.6 = bf16[5376,1024]{1,0:T(8,128)(2,1)} broadcast(bf16[5376]{0:T(1024)(128)(2,1)S(1)} %pad.2), dimensions={0} | broadcast | bytes 11020800 | tf_op jit(solution)/shard_map/cond/branch_1_fun/jit(_pad)/pad | solution.py:160
  164.6 20.5 %dynamic_update_slice.3 = bf16[5376,1024]{1,0:T(8,128)(2,1)} dynamic-update-slice(bf16[5376,1024]{1,0:T(8,128)(2,1)} %pad.6, bf16[2048,1024]{1,0:T(8,128)(2,1)} %select_add_fusion, s32[]{:T(128)S(6)} %min.4, s32[]{:T(128)} %constant.210.clone) | dynamic-update-slice | bytes 8388612 | tf_op jit(solution)/shard_map/cond/branch_1_fun/dynamic_update_slice | solution.py:163
  (163 shorter events, 58.6 us)
Async XLA Ops:
  7.2 9.0 %copy-start.6 = (f32[128]{0:T(128)S(1)}, f32[128]{0:T(128)}, u32[]{:S(2)}) copy-start(f32[128]{0:T(128)} %param.18) | copy-start | bytes 1540
  7.2 86.6 %all-gather.2.cloned.1.call-start = ((), (), s32[]{:S(2)}) async-start(), calls=%async_computation | async-start | bytes 4456448 | tf_op jit(solution)/shard_map/all_gather | solution.py:126
  10.2 6.2 %collective-permute-start.1 = (s32[4]{0:T(128)S(1)}, s32[4]{0:T(128)S(1)}, u32[]{:S(2)}, u32[]{:S(2)}) collective-permute-start(s32[4]{0:T(128)S(1)} %gather_fusion.4), channel_id=1, source_target_pairs={{0,1},{1,0},{2,3},{3,2},{4,5},{5,4},{6,7},{7,6},{8,9},{9,8},{10,11... | collective-permute-start | bytes 56 | tf_op jit(solution)/shard_map/ppermute | solution.py:21
  10.8 12.7 %collective-permute-start = (s32[4,16]{1,0:T(4,128)S(1)}, s32[4,16]{1,0:T(4,128)S(1)}, u32[]{:S(2)}, u32[]{:S(2)}) collective-permute-start(s32[4,16]{1,0:T(4,128)S(1)} %gather_fusion.2), channel_id=1, source_target_pairs={{0,1},{1,0},{2,3},{3,2},{4,5},{5,4},{6,7},{7,6},{8,9},{9,8},{10,11... | collective-permute-start | bytes 776 | tf_op jit(solution)/shard_map/ppermute | solution.py:21
  15.9 18.8 %copy-start.2 = (bf16[128,512]{1,0:T(8,128)(2,1)S(1)}, bf16[128,512]{1,0:T(8,128)(2,1)}, u32[]{:S(2)}) copy-start(bf16[128,512]{1,0:T(8,128)(2,1)} %param.16) | copy-start | bytes 393220
  16.2 19.2 %copy-start.1 = (bf16[128,4096]{1,0:T(8,128)(2,1)S(1)}, bf16[128,4096]{1,0:T(8,128)(2,1)}, u32[]{:S(2)}) copy-start(bf16[128,4096]{1,0:T(8,128)(2,1)} %param.14) | copy-start | bytes 3145732
  18.8 3.5 %collective-permute-start.3 = (s32[4]{0:T(128)S(1)}, s32[4]{0:T(128)S(1)}, u32[]{:S(2)}, u32[]{:S(2)}) collective-permute-start(s32[4]{0:T(128)S(1)} %gather_fusion.8), channel_id=1, source_target_pairs={{0,2},{2,0},{1,3},{3,1},{4,6},{6,4},{5,7},{7,5},{8,10},{10,8},{9,1... | collective-permute-start | bytes 56 | tf_op jit(solution)/shard_map/ppermute | solution.py:21
  24.1 3.6 %collective-permute-start.2 = (s32[4,16]{1,0:T(4,128)S(1)}, s32[4,16]{1,0:T(4,128)S(1)}, u32[]{:S(2)}, u32[]{:S(2)}) collective-permute-start(s32[4,16]{1,0:T(4,128)S(1)} %gather_fusion.6), channel_id=1, source_target_pairs={{0,2},{2,0},{1,3},{3,1},{4,6},{6,4},{5,7},{7,5},{8,10},{10,8},{9,1... | collective-permute-start | bytes 776 | tf_op jit(solution)/shard_map/ppermute | solution.py:21
  28.3 3.6 %collective-permute-start.4 = (s32[4,16]{1,0:T(4,128)S(1)}, s32[4,16]{1,0:T(4,128)S(1)}, u32[]{:S(2)}, u32[]{:S(2)}) collective-permute-start(s32[4,16]{1,0:T(4,128)S(1)} %gather_fusion.10), channel_id=1, source_target_pairs={{0,4},{4,0},{1,5},{5,1},{2,6},{6,2},{3,7},{7,3},{8,12},{12,8},{9,1... | collective-permute-start | bytes 776 | tf_op jit(solution)/shard_map/ppermute | solution.py:21
  36.0 0.7 copy-start.4
  40.9 2.1 %collective-permute-start.5 = (bf16[4,16,4096]{2,1,0:T(8,128)(2,1)}, bf16[4,16,4096]{2,1,0:T(8,128)(2,1)S(1)}, u32[]{:S(2)}, u32[]{:S(2)}) collective-permute-start(bf16[4,16,4096]{2,1,0:T(8,128)(2,1)} %gather_fusion.13), channel_id=1, source_target_pairs={{0,1},{1,0},{2,3},{3,2},{4,5},{5,4},{6,7},{7,6},{8,9},{9,8},{10,11... | collective-permute-start | bytes 1572872 | tf_op jit(solution)/shard_map/ppermute | solution.py:21
  43.7 16.8 %collective-permute-start.6 = (bf16[4,16,4096]{2,1,0:T(8,128)(2,1)S(1)}, bf16[4,16,4096]{2,1,0:T(8,128)(2,1)S(1)}, u32[]{:S(2)}, u32[]{:S(2)}) collective-permute-start(bf16[4,16,4096]{2,1,0:T(8,128)(2,1)S(1)} %gather_fusion.15), channel_id=1, source_target_pairs={{0,2},{2,0},{1,3},{3,1},{4,6},{6,4},{5,7},{7,5},{8,10},{10,8},{9,1... | collective-permute-start | bytes 1572872 | tf_op jit(solution)/shard_map/ppermute | solution.py:21
  44.4 17.8 %copy-start.5 = (s32[16]{0:T(128)S(1)}, s32[16]{0:T(128)}, u32[]{:S(2)}) copy-start(s32[16]{0:T(128)} %param.21) | copy-start | bytes 196
  61.1 26.7 %collective-permute-start.7 = (bf16[4,16,4096]{2,1,0:T(8,128)(2,1)S(1)}, bf16[4,16,4096]{2,1,0:T(8,128)(2,1)S(1)}, u32[]{:S(2)}, u32[]{:S(2)}) collective-permute-start(bf16[4,16,4096]{2,1,0:T(8,128)(2,1)S(1)} %gather_fusion.17), channel_id=1, source_target_pairs={{0,4},{4,0},{1,5},{5,1},{2,6},{6,2},{3,7},{7,3},{8,12},{12,8},{9,1... | collective-permute-start | bytes 1572872 | tf_op jit(solution)/shard_map/ppermute | solution.py:21
  93.8 1.0 copy-start.3
  187.1 1.5 copy-start
Sparse Core Ops, SparseCore 0:
  35.5 58.1 all-gather.1
where the time goes:
time: 197 us; the launch traced here: 195 us
  local copies, waits for them, and re-layouts  64.1 us (33%)
  waiting for transfers between devices  51.9 us (26%)
  other arithmetic  35.1 us (18%)
  matrix products  25.3 us (13%)
  between operations  15.8 us (8%)
  starting transfers between devices  3.12 us (2%)
    ppermute x8, waiting for transfers between devices, partner(): return lax.ppermute(block, axis, route)  46 us
    dynamic_update_slice x1, local copies, waits for them, and re-layouts, place(): padded = lax.dynamic_update_slice_in_dim(padded, region + masked, at, 0)  20.5 us
    dot_general x4, matrix products, absorb(): jnp.einsum('kgqn,nkd->kgqd', probs.astype(jnp.bfloat16), v_blk, preferred...  19.8 us
    reduce_sum x4, other arithmetic, absorb(): total = total * factor + jnp.sum(probs, axis=-1)  8.44 us
    all_gather x1, waiting for transfers between devices, body(): piece = lax.all_gather(key_vals, 'ctx', axis=0, tiled=True)  5.86 us
    dynamic_slice x8, local copies, waits for them, and re-layouts, attend(): lax.scan(absorb, state, (k_part, v_part, k_rows.reshape(blocks, width), p...  5.66 us
    dot_general x4, matrix products, absorb(): jnp.einsum('qkgd,nkd->kgqn', query_heads, k_blk, preferred_element_type=j...  5.49 us
    pad x2, local copies, waits for them, and re-layouts, place(): padded = jnp.pad(stored, ((count, count), (0, 0)))  4.95 us
  transfers between devices with their start and end apart: 9, of which 7 were waited for; matrix products, arithmetic and copies ran while one was open for 11% of the time, Pallas kernels for 0%

commit v1 on v0

v1 whole, which is shorter than its diff:
```python
import functools
import math

import jax
import jax.numpy as jnp
import numpy as np
from jax import lax
from jax.experimental import pallas as pl
from jax.experimental.pallas import tpu as pltpu
from jax.sharding import PartitionSpec as P

HD = 128
TRADE = 8
PLANE = 4
EPS = 1e-06
THETA = 1000000.0
MESH = pl.DeviceIdType.MESH
BF16 = jnp.bfloat16
F32 = jnp.float32


def kernel(
    devices, reach, lead,
    q_ref, k_ref, v_ref, qg_ref, kg_ref, freq_ref, len_ref, place_ref, owner_ref,
    out_ref, cache_ref,
    buf, qrot, bias, stage, obuf,
    rsem, ssem, orecv, osend, csem, lsem,
):
    rows = q_ref.shape[0]
    q_heads = q_ref.shape[1] // HD
    kv_heads = k_ref.shape[1] // HD
    group = q_heads // kv_heads
    unit = rows // TRADE
    tables = len_ref.shape[0]
    back = reach // PLANE
    planes = devices // PLANE
    span = (reach + 1) * rows
    kept = (reach + lead + 1) * rows
    wide = group * HD

    me = lax.axis_index("ctx")
    plane = me // PLANE
    lane = me % PLANE
    across = lane + 2 - 4 * (lane // 2)
    beside = lane + 1 - 2 * (lane % 2)
    corner = across + 1 - 2 * (across % 2)
    here = plane * PLANE
    base = me // TRADE * TRADE
    slot = me % TRADE

    barrier = pltpu.get_barrier_semaphore()
    for step in range(1, TRADE):
        pl.semaphore_signal(
            barrier, inc=1, device_id={"ctx": base + (slot + step) % TRADE}, device_id_type=MESH
        )
    odd = plane % 2
    outer = me + PLANE * (2 * odd - 1)
    has_outer = (outer >= 0) & (outer < devices)

    @pl.when(has_outer)
    def _():
        pl.semaphore_signal(barrier, inc=1, device_id={"ctx": outer}, device_id_type=MESH)

    starts = []
    ends = []
    at = jnp.int32(0)
    for i in range(tables):
        starts.append(at)
        at = at + len_ref[i]
        ends.append(at)
    low = lax.broadcasted_iota(jnp.int32, (rows, HD), 1) < HD // 2

    def start_of(row):
        found = jnp.zeros(row.shape, jnp.int32)
        for i in range(tables):
            found = jnp.where(row >= starts[i], starts[i], found)
        return found

    def turns(row, start):
        angles = (row - start).astype(F32) * freq_ref[...]
        cosine = jnp.cos(angles)
        sine = jnp.sin(angles)
        return cosine, jnp.where(low, -sine, sine)

    def rotate(x, gain, turn):
        mean_sq = jnp.mean(x * x, axis=-1, keepdims=True)
        y = x * lax.rsqrt(mean_sq + EPS) * gain
        return (y * turn[0] + pltpu.roll(y, HD // 2, 1) * turn[1]).astype(BF16)

    local = lax.broadcasted_iota(jnp.int32, (rows, HD), 0)
    own_rows = me * rows + local
    k_turn = turns(own_rows, start_of(own_rows))

    own_at = pl.multiple_of((back * PLANE + lane) * rows, rows)
    for h in range(kv_heads):
        buf[h, pl.ds(own_at, rows), 0:HD] = rotate(
            k_ref[:, h * HD:(h + 1) * HD].astype(F32), kg_ref[...], k_turn
        )
        buf[h, pl.ds(own_at, rows), HD:2 * HD] = v_ref[:, h * HD:(h + 1) * HD]

    def has(k):
        if k == back + 1:
            return plane + 1 < planes
        return plane >= back - k

    depth = PLANE * rows
    for k in range(back + 2):
        if k != back:
            @pl.when(jnp.logical_not(has(k)))
            def _(k=k):
                for h in range(kv_heads):
                    buf[h, k * depth:(k + 1) * depth, :] = jnp.zeros((depth, 2 * HD), BF16)

    @pl.when(has_outer)
    def _():
        pl.semaphore_wait(barrier, TRADE)

    @pl.when(jnp.logical_not(has_outer))
    def _():
        pl.semaphore_wait(barrier, TRADE - 1)

    def piece(h, k, j):
        return buf.at[h, pl.ds(pl.multiple_of((k * PLANE + j) * rows, rows), rows), :]

    def send(h, k, j, kind, to_k, device):
        return pltpu.make_async_remote_copy(
            src_ref=piece(h, k, j),
            dst_ref=piece(h, to_k, j),
            send_sem=ssem.at[h, k, kind],
            recv_sem=rsem.at[h, to_k, j],
            device_id={"ctx": device},
            device_id_type=MESH,
        )

    def line(h, k):
        return send(h, k, lane, 0, k - 1, me + PLANE)

    def down(h):
        return send(h, back, lane, 4, back + 1, me - PLANE)

    def over(h, k):
        return send(h, k, lane, 1, k, here + across)

    def near(h, k):
        return send(h, k, lane, 2, k, here + beside)

    def pass_on(h, k):
        return send(h, k, across, 3, k, here + beside)

    def arrive(h, k, j):
        send(h, k, j, 0, k, here + beside).wait_recv()

    can_up = plane + 1 < planes
    can_down = (plane > 0) & (lane < lead)

    def carried(k, j):
        return has(k) & (j < lead) if k == back + 1 else has(k)

    def launch_own(h):
        @pl.when(can_up)
        def _():
            line(h, back).start()

        over(h, back).start()
        near(h, back).start()

        @pl.when(can_down)
        def _():
            down(h).start()

    order = [back + 1] + list(range(back - 1, -1, -1))

    def forward(h):
        for k in order:
            @pl.when(carried(k, lane))
            def _(k=k):
                arrive(h, k, lane)
                if 1 <= k <= back:
                    @pl.when(can_up)
                    def _():
                        line(h, k).start()
                over(h, k).start()
                near(h, k).start()
        for k in [back] + order:
            @pl.when(carried(k, across))
            def _(k=k):
                arrive(h, k, across)
                pass_on(h, k).start()

    def gather(h):
        for k in [back] + order:
            for j in (beside, corner):
                @pl.when(carried(k, j))
                def _(k=k, j=j):
                    arrive(h, k, j)

    for h in range(kv_heads):
        launch_own(h)

    source = jnp.zeros((rows, HD), jnp.int32)
    for u in range(TRADE):
        found = jnp.int32(0)
        for j in range(TRADE):
            found = found + jnp.where(place_ref[0, j] == base + u, j, 0)
        source = jnp.where(local // unit == u, found * unit + local % unit, source)
    column = lax.broadcasted_iota(jnp.int32, (rows, HD), 1)
    picks = jnp.where(source == column, 1.0, 0.0).astype(BF16)
    q_rows = me * rows + source
    q_start = start_of(q_rows)
    q_turn = turns(q_rows, q_start)

    def turn_head(i, unused):
        cols = pl.ds(pl.multiple_of(i * HD, HD), HD)
        x = jnp.dot(picks, q_ref[:, cols], preferred_element_type=F32)
        qrot[pl.ds(pl.multiple_of(i * rows, rows), rows), :] = rotate(x, qg_ref[...], q_turn)
        return unused

    lax.fori_loop(0, q_heads, turn_head, 0)

    for b in range(reach + 1):
        c = (me - reach + b) * rows + column
        ok = (c >= q_start) & (c <= q_rows)
        bias[:, b * rows:(b + 1) * rows] = jnp.where(ok, 0.0, -1e30)

    log2_scale = math.log2(math.e) / math.sqrt(HD)
    first = pl.multiple_of(lane * rows, rows)
    chunk = 2

    def attend(h):
        def some(n, unused):
            q = qrot[pl.ds(pl.multiple_of((h * group + n * chunk) * rows, rows), chunk * rows), :]
            s = lax.dot_general(
                q, buf[h, pl.ds(first, span), 0:HD], (((1,), (1,)), ((), ())),
                preferred_element_type=F32,
            )
            s = s.reshape(chunk, rows, span) * log2_scale + bias[...][None]
            prob = jnp.exp2(s - jnp.max(s, axis=-1, keepdims=True))
            total = jnp.sum(prob, axis=-1, keepdims=True)
            mixed = jnp.dot(
                prob.astype(BF16).reshape(chunk * rows, span),
                buf[h, pl.ds(first, span), HD:2 * HD],
                preferred_element_type=F32,
            )
            done = (mixed.reshape(chunk, rows, HD) / total).astype(BF16)
            for g in range(chunk):
                cols = pl.ds(pl.multiple_of((n * chunk + g) * HD, HD), HD)
                obuf[h, :, cols] = done[g]
            return unused

        lax.fori_loop(0, group // chunk, some, 0)

    def result(h, u):
        return pltpu.make_async_remote_copy(
            src_ref=obuf.at[h, pl.ds(u * unit, unit), :],
            dst_ref=out_ref.at[pl.ds(slot * unit, unit), pl.ds(h * wide, wide)],
            send_sem=osend.at[h, u],
            recv_sem=orecv.at[h, slot],
            device_id={"ctx": base + u},
            device_id_type=MESH,
        )

    def own_result(h):
        return pltpu.make_async_copy(
            obuf.at[h, pl.ds(slot * unit, unit), :],
            out_ref.at[pl.ds(slot * unit, unit), pl.ds(h * wide, wide)],
            lsem.at[h],
        )

    def trade(h):
        for u in range(TRADE):
            @pl.when(slot != u)
            def _(u=u):
                result(h, u).start()
        own_result(h).start()

    def cache_copy(h, part):
        return pltpu.make_async_copy(
            stage.at[h, part],
            cache_ref.at[:, pl.ds((part * kv_heads + h) * HD, HD)],
            csem.at[h, part],
        )

    def keep(h):
        for b in range(reach + lead + 1):
            r = (me - reach + b) * rows + lax.broadcasted_iota(jnp.int32, (rows, HD), 0)
            kept_rows = jnp.zeros((rows, HD), jnp.int32)
            for i in range(tables):
                held = jnp.where(owner_ref[i] == me, 1, 0)
                kept_rows = jnp.where(r >= starts[i], held, kept_rows)
            kept_rows = kept_rows * jnp.where((r >= 0) & (r < devices * rows), 1, 0)
            flag = kept_rows.astype(F32)
            at = pl.ds(pl.multiple_of((lane + b) * rows, rows), rows)
            for part in range(2):
                data = buf[h, at, part * HD:(part + 1) * HD].astype(F32)
                stage[h, part, b * rows:(b + 1) * rows, :] = jnp.where(
                    flag > 0.5, data, 0.0
                ).astype(BF16)
        for part in range(2):
            cache_copy(h, part).start()

    forward(0)
    for h in range(kv_heads):
        if h + 1 < kv_heads:
            forward(h + 1)
        gather(h)
        attend(h)
        trade(h)
        keep(h)

    for h in range(kv_heads):
        @pl.when(can_up)
        def _(h=h):
            line(h, back).wait_send()

        over(h, back).wait_send()
        near(h, back).wait_send()

        @pl.when(can_down)
        def _(h=h):
            down(h).wait_send()

        for k in order:
            @pl.when(carried(k, lane))
            def _(h=h, k=k):
                if 1 <= k <= back:
                    @pl.when(can_up)
                    def _():
                        line(h, k).wait_send()
                over(h, k).wait_send()
                near(h, k).wait_send()
        for k in [back] + order:
            @pl.when(carried(k, across))
            def _(h=h, k=k):
                pass_on(h, k).wait_send()
        own_result(h).wait()
        for part in range(2):
            cache_copy(h, part).wait()
        for u in range(TRADE):
            @pl.when(slot != u)
            def _(h=h, u=u):
                result(h, u).wait_send()
                pltpu.make_async_remote_copy(
                    src_ref=obuf.at[h, pl.ds(u * unit, unit), :],
                    dst_ref=out_ref.at[pl.ds(u * unit, unit), pl.ds(h * wide, wide)],
                    send_sem=osend.at[h, u],
                    recv_sem=orecv.at[h, u],
                    device_id={"ctx": base + u},
                    device_id_type=MESH,
                ).wait_recv()


def body(queries, keys, values, q_gain, k_gain, lengths, placing, owners):
    rows = queries.shape[0]
    q_heads = queries.shape[1] // HD
    kv_heads = keys.shape[1] // HD
    group = q_heads // kv_heads
    devices = lax.axis_size("ctx")
    reach = devices // 2
    lead = devices // 16
    planes = reach // PLANE + 2
    kept = (reach + lead + 1) * rows
    freqs = np.power(THETA, -np.arange(0, HD, 2) / HD).astype(np.float32)
    freqs = jnp.asarray(np.concatenate([freqs, freqs])[None, :])
    vmem = pl.BlockSpec(memory_space=pltpu.VMEM)
    smem = pl.BlockSpec(memory_space=pltpu.SMEM)
    hbm = pl.BlockSpec(memory_space=pl.ANY)
    dma = pltpu.SemaphoreType.DMA
    return pl.pallas_call(
        functools.partial(kernel, devices, reach, lead),
        out_shape=(
            jax.ShapeDtypeStruct(queries.shape, BF16),
            jax.ShapeDtypeStruct((kept, 2 * keys.shape[1]), BF16),
        ),
        in_specs=[vmem] * 6 + [smem] * 3,
        out_specs=(hbm, hbm),
        scratch_shapes=[
            pltpu.VMEM((kv_heads, planes * PLANE * rows, 2 * HD), BF16),
            pltpu.VMEM((q_heads * rows, HD), BF16),
            pltpu.VMEM((rows, (reach + 1) * rows), F32),
            pltpu.VMEM((kv_heads, 2, kept, HD), BF16),
            pltpu.VMEM((kv_heads, rows, group * HD), BF16),
            dma((kv_heads, planes, PLANE)),
            dma((kv_heads, planes, 5)),
            dma((kv_heads, TRADE)),
            dma((kv_heads, TRADE)),
            dma((kv_heads, 2)),
            dma((kv_heads,)),
        ],
        compiler_params=pltpu.CompilerParams(
            collective_id=0, has_side_effects=True, vmem_limit_bytes=56 * 2**20
        ),
    )(
        queries, keys, values, q_gain[None, :], k_gain[None, :], freqs,
        lengths, placing, owners,
    )


def solution(mesh):
    return jax.shard_map(
        body,
        mesh=mesh,
        in_specs=(
            P(("groups", "ctx"), None),
            P(("groups", "ctx"), None),
            P(("groups", "ctx"), None),
            P(),
            P(),
            P("groups"),
            P(("groups", "ctx"), None),
            P("groups"),
        ),
        out_specs=(P(("groups", "ctx"), None), P(("groups", "ctx"), None)),
        check_vma=False,
    )
```

time: 197 us -> 66 us (0.34)
  the two profiles are of different devices: /device:TPU:12 before, /device:TPU:21 now
where the time goes in v1:
time: 66 us; the launch traced here: 65.8 us
  Pallas kernels  59.4 us (90%)
  local copies, waits for them, and re-layouts  5.76 us (9%)
    pallas_call x1, Pallas kernels, body(): pl.pallas_call(functools.partial(kernel, devices, reach, lead), out_shape...  59.4 us
    unnamed x2, local copies, waits for them, and re-layouts  5.76 us

profile of v1, /device:TPU:21, one launch (start us, length us, event | category | flops | bytes accessed | tf_op | source)
XLA Modules:
  0.0 65.8 jit_solution(8409993527192242833)
XLA Ops:
  0.6 59.4 %shard_map.104 = (bf16[128,4096]{1,0:T(8,128)(2,1)}, bf16[1280,1024]{1,0:T(8,128)(2,1)}) custom-call(bf16[128,4096]{1,0:T(8,128)(2,1)} %q_ref.1, bf16[128,512]{1,0:T(8,128)(2,1)} %k_ref.1, bf16[128,512]{1,0:T(8,128)(2,1)} %v_ref.1, f32[1,128]{1,0:T(1,128)} %bitcast.2, f32[1,128]{1,0:T(1,128)} %bitcast.3, f32[1,128]{1,0:T(1,128)} %constant.2.clone.freq_ref, ...), custom_call_target="tpu_custom_call" | custom-call | tf_op jit(solution)/shard_map/pallas_call | solution.py:368
  60.1 2.3 %copy.13 = bf16[128,4096]{1,0:T(8,128)(2,1)} copy(bf16[128,4096]{1,0:T(8,128)(2,1)} %get-tuple-element.4) | data formatting | bytes 2097152
  62.4 3.5 %copy.14 = bf16[1280,1024]{1,0:T(8,128)(2,1)} copy(bf16[1280,1024]{1,0:T(8,128)(2,1)} %get-tuple-element.5) | data formatting | bytes 5242880

commit v2 on v1

--- a/solution.py
+++ b/solution.py
@@ -12,6 +12,7 @@
 HD = 128
 TRADE = 8
 PLANE = 4
+STAGES = 2
 EPS = 1e-06
 THETA = 1000000.0
 MESH = pl.DeviceIdType.MESH
@@ -23,8 +24,8 @@
     devices, reach, lead,
     q_ref, k_ref, v_ref, qg_ref, kg_ref, freq_ref, len_ref, place_ref, owner_ref,
     out_ref, cache_ref,
-    buf, qrot, bias, stage, obuf,
-    rsem, ssem, orecv, osend, csem, lsem,
+    buf, qrot, bias, owned, obuf,
+    rsem, ssem, orecv, osend, lsem,
 ):
     rows = q_ref.shape[0]
     q_heads = q_ref.shape[1] // HD
@@ -37,6 +38,7 @@
     span = (reach + 1) * rows
     kept = (reach + lead + 1) * rows
     wide = group * HD
+    per = kv_heads // STAGES
 
     me = lax.axis_index("ctx")
     plane = me // PLANE
@@ -120,7 +122,7 @@
         pl.semaphore_wait(barrier, TRADE - 1)
 
     def piece(h, k, j):
-        return buf.at[h, pl.ds(pl.multiple_of((k * PLANE + j) * rows, rows), rows), :]
+        return buf.at[pl.ds(h * per, per), pl.ds(pl.multiple_of((k * PLANE + j) * rows, rows), rows), :]
 
     def send(h, k, j, kind, to_k, device):
         return pltpu.make_async_remote_copy(
@@ -168,24 +170,35 @@
         def _():
             down(h).start()
 
-    order = [back + 1] + list(range(back - 1, -1, -1))
+    order = list(range(back - 1, -1, -1)) + [back + 1]
+
+    def take(h, k):
+        @pl.when(carried(k, lane))
+        def _():
+            arrive(h, k, lane)
+            if 1 <= k <= back:
+                @pl.when(can_up)
+                def _():
+                    line(h, k).start()
+            over(h, k).start()
+            near(h, k).start()
+
+    def hand(h, k):
+        @pl.when(carried(k, across))
+        def _():
+            arrive(h, k, across)
+            pass_on(h, k).start()
+
+    def relay(h):
+        take(h, back - 1)
+        hand(h, back)
 
     def forward(h):
         for k in order:
-            @pl.when(carried(k, lane))
-            def _(k=k):
-                arrive(h, k, lane)
-                if 1 <= k <= back:
-                    @pl.when(can_up)
-                    def _():
-                        line(h, k).start()
-                over(h, k).start()
-                near(h, k).start()
-        for k in [back] + order:
-            @pl.when(carried(k, across))
-            def _(k=k):
-                arrive(h, k, across)
-                pass_on(h, k).start()
+            if k != back - 1:
+                take(h, k)
+        for k in order:
+            hand(h, k)
 
     def gather(h):
         for k in [back] + order:
@@ -194,8 +207,14 @@
                 def _(k=k, j=j):
                     arrive(h, k, j)
 
-    for h in range(kv_heads):
-        launch_own(h)
+    def loop(step, count=STAGES):
+        def at(h, unused):
+            step(h)
+            return unused
+
+        lax.fori_loop(0, count, at, 0)
+
+    loop(launch_own)
 
     source = jnp.zeros((rows, HD), jnp.int32)
     for u in range(TRADE):
@@ -207,20 +226,34 @@
     picks = jnp.where(source == column, 1.0, 0.0).astype(BF16)
     q_rows = me * rows + source
     q_start = start_of(q_rows)
-    q_turn = turns(q_rows, q_start)
 
     def turn_head(i, unused):
         cols = pl.ds(pl.multiple_of(i * HD, HD), HD)
-        x = jnp.dot(picks, q_ref[:, cols], preferred_element_type=F32)
-        qrot[pl.ds(pl.multiple_of(i * rows, rows), rows), :] = rotate(x, qg_ref[...], q_turn)
+        x = rotate(q_ref[:, cols].astype(F32), qg_ref[...], k_turn)
+        x = jnp.dot(picks, x, preferred_element_type=F32)
+        qrot[pl.ds(pl.multiple_of(i * rows, rows), rows), :] = x.astype(BF16)
         return unused
 
-    lax.fori_loop(0, q_heads, turn_head, 0)
+    lax.fori_loop(0, q_heads, turn_head, 0, unroll=8)
+    loop(relay)
 
     for b in range(reach + 1):
         c = (me - reach + b) * rows + column
         ok = (c >= q_start) & (c <= q_rows)
         bias[:, b * rows:(b + 1) * rows] = jnp.where(ok, 0.0, -1e30)
+
+    holds = [jnp.where(owner_ref[i] == me, 1, 0) for i in range(tables)]
+
+    def own_block(b, unused):
+        r = (me - reach + b) * rows + local
+        flag = jnp.zeros((rows, HD), jnp.int32)
+        for i in range(tables):
+            flag = jnp.where(r >= starts[i], holds[i], flag)
+        flag = flag * jnp.where((r >= 0) & (r < devices * rows), 1, 0)
+        owned[pl.ds(pl.multiple_of(b * rows, rows), rows), :] = flag.astype(F32).astype(BF16)
+        return unused
+
+    lax.fori_loop(0, reach + lead + 1, own_block, 0)
 
     log2_scale = math.log2(math.e) / math.sqrt(HD)
     first = pl.multiple_of(lane * rows, rows)
@@ -273,55 +306,44 @@
                 result(h, u).start()
         own_result(h).start()
 
-    def cache_copy(h, part):
-        return pltpu.make_async_copy(
-            stage.at[h, part],
-            cache_ref.at[:, pl.ds((part * kv_heads + h) * HD, HD)],
-            csem.at[h, part],
-        )
-
     def keep(h):
-        for b in range(reach + lead + 1):
-            r = (me - reach + b) * rows + lax.broadcasted_iota(jnp.int32, (rows, HD), 0)
-            kept_rows = jnp.zeros((rows, HD), jnp.int32)
-            for i in range(tables):
-                held = jnp.where(owner_ref[i] == me, 1, 0)
-                kept_rows = jnp.where(r >= starts[i], held, kept_rows)
-            kept_rows = kept_rows * jnp.where((r >= 0) & (r < devices * rows), 1, 0)
-            flag = kept_rows.astype(F32)
-            at = pl.ds(pl.multiple_of((lane + b) * rows, rows), rows)
-            for part in range(2):
-                data = buf[h, at, part * HD:(part + 1) * HD].astype(F32)
-                stage[h, part, b * rows:(b + 1) * rows, :] = jnp.where(
-                    flag > 0.5, data, 0.0
-                ).astype(BF16)
+        data = buf[h, pl.ds(first, kept), :]
         for part in range(2):
-            cache_copy(h, part).start()
+            half = data[:, part * HD:(part + 1) * HD]
+            cols = pl.ds(pl.multiple_of((part * kv_heads + h) * HD, HD), HD)
+            cache_ref[:, cols] = half * owned[...]
 
     forward(0)
-    for h in range(kv_heads):
-        if h + 1 < kv_heads:
+
+    def stage_of(h):
+        @pl.when(h + 1 < STAGES)
+        def _():
             forward(h + 1)
+
         gather(h)
-        attend(h)
-        trade(h)
-        keep(h)
-
-    for h in range(kv_heads):
+        for i in range(per):
+            attend(h * per + i)
+            trade(h * per + i)
+        for i in range(per):
+            keep(h * per + i)
+
+    loop(stage_of)
+
+    def finish(h):
         @pl.when(can_up)
-        def _(h=h):
+        def _():
             line(h, back).wait_send()
 
         over(h, back).wait_send()
         near(h, back).wait_send()
 
         @pl.when(can_down)
-        def _(h=h):
+        def _():
             down(h).wait_send()
 
         for k in order:
             @pl.when(carried(k, lane))
-            def _(h=h, k=k):
+            def _(k=k):
                 if 1 <= k <= back:
                     @pl.when(can_up)
                     def _():
@@ -330,14 +352,14 @@
                 near(h, k).wait_send()
         for k in [back] + order:
             @pl.when(carried(k, across))
-            def _(h=h, k=k):
+            def _(k=k):
                 pass_on(h, k).wait_send()
+
+    def finish_trade(h):
         own_result(h).wait()
-        for part in range(2):
-            cache_copy(h, part).wait()
         for u in range(TRADE):
             @pl.when(slot != u)
-            def _(h=h, u=u):
+            def _(u=u):
                 result(h, u).wait_send()
                 pltpu.make_async_remote_copy(
                     src_ref=obuf.at[h, pl.ds(u * unit, unit), :],
@@ -347,6 +369,9 @@
                     device_id={"ctx": base + u},
                     device_id_type=MESH,
                 ).wait_recv()
+
+    loop(finish)
+    loop(finish_trade, kv_heads)
 
 
 def body(queries, keys, values, q_gain, k_gain, lengths, placing, owners):
@@ -363,31 +388,29 @@
     freqs = jnp.asarray(np.concatenate([freqs, freqs])[None, :])
     vmem = pl.BlockSpec(memory_space=pltpu.VMEM)
     smem = pl.BlockSpec(memory_space=pltpu.SMEM)
-    hbm = pl.BlockSpec(memory_space=pl.ANY)
     dma = pltpu.SemaphoreType.DMA
     return pl.pallas_call(
         functools.partial(kernel, devices, reach, lead),
         out_shape=(
-            jax.ShapeDtypeStruct(queries.shape, BF16),
-            jax.ShapeDtypeStruct((kept, 2 * keys.shape[1]), BF16),
+            pltpu.VMEM(queries.shape, BF16),
+            pltpu.VMEM((kept, 2 * keys.shape[1]), BF16),
         ),
         in_specs=[vmem] * 6 + [smem] * 3,
-        out_specs=(hbm, hbm),
+        out_specs=(vmem, vmem),
         scratch_shapes=[
             pltpu.VMEM((kv_heads, planes * PLANE * rows, 2 * HD), BF16),
             pltpu.VMEM((q_heads * rows, HD), BF16),
             pltpu.VMEM((rows, (reach + 1) * rows), F32),
-            pltpu.VMEM((kv_heads, 2, kept, HD), BF16),
+            pltpu.VMEM((kept, HD), BF16),
             pltpu.VMEM((kv_heads, rows, group * HD), BF16),
-            dma((kv_heads, planes, PLANE)),
-            dma((kv_heads, planes, 5)),
+            dma((STAGES, planes, PLANE)),
+            dma((STAGES, planes, 5)),
             dma((kv_heads, TRADE)),
             dma((kv_heads, TRADE)),
-            dma((kv_heads, 2)),
             dma((kv_heads,)),
         ],
         compiler_params=pltpu.CompilerParams(
-            collective_id=0, has_side_effects=True, vmem_limit_bytes=56 * 2**20
+            collective_id=0, has_side_effects=True, vmem_limit_bytes=40 * 2**20
         ),
     )(
         queries, keys, values, q_gain[None, :], k_gain[None, :], freqs,

time: 66 us -> 53.6 us (0.81); the launches traced: 65.8 us -> 52.7 us
  Pallas kernels: 59.4 us -> 42.7 us
  local copies, waits for them, and re-layouts: 5.76 us -> 9.42 us
    pallas_call x1, Pallas kernels: 59.4 us -> 42.7 us  [body(): pl.pallas_call(functools.partial(kernel, devices, reach, lead), out_shape...]
    unnamed x2 -> x20, local copies, waits for them, and re-layouts: 5.76 us -> 9.42 us
where the time goes in v2:
time: 53.6 us; the launch traced here: 52.7 us
  Pallas kernels  42.7 us (80%)
  local copies, waits for them, and re-layouts  9.42 us (18%)
  between operations  0.66 us (1%)
    pallas_call x1, Pallas kernels, body(): pl.pallas_call(functools.partial(kernel, devices, reach, lead), out_shape...  42.7 us
    unnamed x20, local copies, waits for them, and re-layouts  9.42 us

profile of v2, /device:TPU:21, one launch (start us, length us, event | category | flops | bytes accessed | tf_op | source)
XLA Modules:
  0.0 52.7 jit_solution(6510646764219885270)
XLA Ops:
  0.6 0.0 copy-start
  0.6 1.2 %copy-done = bf16[128,4096]{1,0:T(8,128)(2,1)S(1)} copy-done((bf16[128,4096]{1,0:T(8,128)(2,1)S(1)}, bf16[128,4096]{1,0:T(8,128)(2,1)}, u32[]{:S(2)}) %copy-start) | copy-done | bytes 1048600
  1.9 0.0 copy-start.1
  1.9 0.9 %copy-done.1 = bf16[128,512]{1,0:T(8,128)(2,1)S(1)} copy-done((bf16[128,512]{1,0:T(8,128)(2,1)S(1)}, bf16[128,512]{1,0:T(8,128)(2,1)}, u32[]{:S(2)}) %copy-start.1) | copy-done | bytes 131096
  2.8 0.0 copy-start.2
  2.8 0.9 %copy-done.2 = bf16[128,512]{1,0:T(8,128)(2,1)S(1)} copy-done((bf16[128,512]{1,0:T(8,128)(2,1)S(1)}, bf16[128,512]{1,0:T(8,128)(2,1)}, u32[]{:S(2)}) %copy-start.2) | copy-done | bytes 131096
  3.7 0.0 copy-start.3
  3.7 0.7 %copy-done.3 = f32[128]{0:T(128)S(1)} copy-done((f32[128]{0:T(128)S(1)}, f32[128]{0:T(128)}, u32[]{:S(2)}) %copy-start.3) | copy-done | bytes 536
  4.3 0.0 copy-start.4
  4.3 0.7 %copy-done.4 = f32[128]{0:T(128)S(1)} copy-done((f32[128]{0:T(128)S(1)}, f32[128]{0:T(128)}, u32[]{:S(2)}) %copy-start.4) | copy-done | bytes 536
  5.0 0.0 copy-start.5
  5.0 0.7 %copy-done.5 = s32[16]{0:T(128)S(1)} copy-done((s32[16]{0:T(128)S(1)}, s32[16]{0:T(128)}, u32[]{:S(2)}) %copy-start.5) | copy-done | bytes 88
  5.6 0.0 copy-start.6
  5.6 0.7 %copy-done.6 = s32[1,8]{1,0:T(1,128)S(1)} copy-done((s32[1,8]{1,0:T(1,128)S(1)}, s32[1,8]{1,0:T(1,128)}, u32[]{:S(2)}) %copy-start.6) | copy-done | bytes 56
  6.3 0.0 copy-start.7
  6.3 0.7 %copy-done.7 = s32[16]{0:T(128)S(1)} copy-done((s32[16]{0:T(128)S(1)}, s32[16]{0:T(128)}, u32[]{:S(2)}) %copy-start.7) | copy-done | bytes 88
  6.9 0.0 copy-start.8
  6.9 0.7 %copy-done.8 = f32[1,128]{1,0:T(1,128)S(1)} copy-done((f32[1,128]{1,0:T(1,128)S(1)}, f32[1,128]{1,0:T(1,128)}, u32[]{:S(2)}) %copy-start.8) | copy-done | bytes 536
  7.6 42.7 %shard_map.104 = (bf16[128,4096]{1,0:T(8,128)(2,1)S(1)}, bf16[1280,1024]{1,0:T(8,128)(2,1)S(1)}) custom-call(bf16[128,4096]{1,0:T(8,128)(2,1)S(1)} %copy-done, bf16[128,512]{1,0:T(8,128)(2,1)S(1)} %copy-done.1, bf16[128,512]{1,0:T(8,128)(2,1)S(1)} %copy-done.2, f32[1,128]{1,0:T(1,128)S(1)} %bitcast.2, f32[1,128]{1,0:T(1,128)S(1)} %bitcast.3, ...), custom_call_target="tpu_custom_call" | custom-call | tf_op jit(solution)/shard_map/pallas_call | solution.py:392
  50.3 1.0 %copy.13 = bf16[128,4096]{1,0:T(8,128)(2,1)} copy(bf16[128,4096]{1,0:T(8,128)(2,1)S(1)} %get-tuple-element.2) | data formatting | bytes 2097152
  51.2 1.5 %copy.14 = bf16[1280,1024]{1,0:T(8,128)(2,1)} copy(bf16[1280,1024]{1,0:T(8,128)(2,1)S(1)} %get-tuple-element.3) | data formatting | bytes 5242880
Async XLA Ops:
  0.6 1.2 %copy-start = (bf16[128,4096]{1,0:T(8,128)(2,1)S(1)}, bf16[128,4096]{1,0:T(8,128)(2,1)}, u32[]{:S(2)}) copy-start(bf16[128,4096]{1,0:T(8,128)(2,1)} %q_ref.1) | copy-start | bytes 3145732
  1.9 0.9 %copy-start.1 = (bf16[128,512]{1,0:T(8,128)(2,1)S(1)}, bf16[128,512]{1,0:T(8,128)(2,1)}, u32[]{:S(2)}) copy-start(bf16[128,512]{1,0:T(8,128)(2,1)} %k_ref.1) | copy-start | bytes 393220
  2.8 0.9 %copy-start.2 = (bf16[128,512]{1,0:T(8,128)(2,1)S(1)}, bf16[128,512]{1,0:T(8,128)(2,1)}, u32[]{:S(2)}) copy-start(bf16[128,512]{1,0:T(8,128)(2,1)} %v_ref.1) | copy-start | bytes 393220
  3.7 0.7 %copy-start.3 = (f32[128]{0:T(128)S(1)}, f32[128]{0:T(128)}, u32[]{:S(2)}) copy-start(f32[128]{0:T(128)} %param.12) | copy-start | bytes 1540
  4.3 0.7 %copy-start.4 = (f32[128]{0:T(128)S(1)}, f32[128]{0:T(128)}, u32[]{:S(2)}) copy-start(f32[128]{0:T(128)} %param.13) | copy-start | bytes 1540
  5.0 0.7 %copy-start.5 = (s32[16]{0:T(128)S(1)}, s32[16]{0:T(128)}, u32[]{:S(2)}) copy-start(s32[16]{0:T(128)} %len_ref.1) | copy-start | bytes 196
  5.6 0.7 %copy-start.6 = (s32[1,8]{1,0:T(1,128)S(1)}, s32[1,8]{1,0:T(1,128)}, u32[]{:S(2)}) copy-start(s32[1,8]{1,0:T(1,128)} %place_ref.1) | copy-start | bytes 100
  6.3 0.7 %copy-start.7 = (s32[16]{0:T(128)S(1)}, s32[16]{0:T(128)}, u32[]{:S(2)}) copy-start(s32[16]{0:T(128)} %owner_ref.1) | copy-start | bytes 196
  6.9 0.7 %copy-start.8 = (f32[1,128]{1,0:T(1,128)S(1)}, f32[1,128]{1,0:T(1,128)}, u32[]{:S(2)}) copy-start(f32[1,128]{1,0:T(1,128)} %constant.2.clone.freq_ref) | copy-start | bytes 1540
